TPU v7x, 512 devices: a whole 4x8x8 slice. The times are simulated.
512 devices in a mesh: stn: 32 (over x, y_lo, core), tm: 16 (over y_hi, z).
Axes of the slice: x: 4, y: 8 (y_hi: 2, y_lo: 4; y = y_hi * 4 + y_lo), z: 8, core: 2. Of those that a mesh axis runs over, the one named last changes fastest.
Arguments:
- samples: bfloat16 [512, 2, 491520], P('stn', None, 'tm'), may hold values from -6 to 6
- filter_taps: float32 [16, 384], replicated, may hold values from -1.5 to 1.5
- frac_delay: float32 [512], P('stn'), may hold values from 0 to 1
- station_delay: int32 [512], P('stn'), may hold values from 0 to 1536, as said below
- beam_index: int32 [500, 512], replicated, may hold values from 0 to 255
Outputs:
- beam_power: float32 [384, 500, 1280], P('stn', None, 'tm')
Inputs may be any that keep to these rules, and one draw needn't show every extreme that they name: `station_delay`: every station's delay lies in 0 to 1536; some station has exactly 1536.
All inputs are finite; a program needn't handle non-finite values.
Results may differ from a plain program's by a relative error of at most 0.0053.
Values may be sent and summed in bfloat16 or wider, within the bound.
A program may use at most 128 MiB of HBM per device.

v0:
```python
import math

import jax
import jax.numpy as jnp
from jax import lax
from jax.sharding import PartitionSpec as P

DSPEC = 4


def from_behind(value, axis, steps):
    count = lax.axis_size(axis)
    initial, last = (max(0, -steps), min(count, count - steps))
    return lax.ppermute(value, axis, [(source, source + steps) for source in range(initial, last)])


def dft_table(width):
    counter = jnp.arange(width, dtype=jnp.int32)
    product = counter[:, None] * counter[None, :] % width
    angle = 2.0 * math.pi / width * product.astype(jnp.float32)
    factor = 1.0 / math.sqrt(width)
    cosine = jnp.cos(angle) * factor
    sine = jnp.sin(angle) * factor
    upper = jnp.concatenate([cosine, -sine], axis=1)
    lower = jnp.concatenate([sine, cosine], axis=1)
    return jnp.concatenate([upper, lower], axis=0).astype(jnp.bfloat16)


def polyphase(delayed, filter_taps, table, frac_delay):
    stations = delayed.shape[0]
    taps, width = filter_taps.shape
    spectra = delayed.shape[2] // width - taps + 1
    blocks = delayed.reshape(stations, 2, spectra + taps - 1, width)
    summed = jnp.zeros((stations, 2, spectra, width), jnp.float32)
    for tap_index in range(taps):
        summed = (
            summed
            + blocks[:, :, tap_index : tap_index + spectra, :].astype(jnp.float32)
            * filter_taps[tap_index]
        )
    frames = (
        summed.astype(jnp.bfloat16).transpose(0, 2, 1, 3).reshape(stations * spectra, 2 * width)
    )
    spectrum = jnp.dot(frames, table, preferred_element_type=jnp.float32).reshape(
        stations, spectra, 2, width
    )
    offsets = (jnp.arange(width, dtype=jnp.int32) - width // 2).astype(jnp.float32)
    phase = 2.0 * math.pi / width * frac_delay[:, None] * offsets[None, :]
    cosine = jnp.cos(phase)[:, None, :]
    sine = jnp.sin(phase)[:, None, :]
    real_part = spectrum[:, :, 0, :]
    imag_part = spectrum[:, :, 1, :]
    rotated_re = real_part * cosine - imag_part * sine
    rotated_im = real_part * sine + imag_part * cosine
    return jnp.stack([rotated_re, rotated_im], axis=1).astype(jnp.bfloat16)


def detect_beams(beam_index, channel, data, width, spectra):
    product = beam_index * (channel - width // 2) % (16 * width)
    angle = 2.0 * math.pi / (16 * width) * product.astype(jnp.float32)
    weight_re = jnp.cos(angle).astype(jnp.bfloat16)
    weight_im = jnp.sin(angle).astype(jnp.bfloat16)
    first = jnp.dot(weight_re, data, preferred_element_type=jnp.float32)
    second = jnp.dot(weight_im, data, preferred_element_type=jnp.float32)
    beam_re = first[:, :spectra] - second[:, spectra:]
    beam_im = first[:, spectra:] + second[:, :spectra]
    return (beam_re * beam_re + beam_im * beam_im) / beam_index.shape[1]


def slice_rows(extended, starts, length):
    return jax.vmap(
        lambda station_row, start_value: lax.dynamic_slice_in_dim(
            station_row, start_value, length, 1
        )
    )(extended, starts)


def local(samples, filter_taps, frac_delay, station_delay, beam_index):
    taps, width = filter_taps.shape
    spectra = samples.shape[2] // width
    table = dft_table(width)
    length = (spectra + taps - 1) * width
    reach = (taps - 1 + DSPEC) * width
    rim_block = from_behind(samples[:, :, :reach], "tm", -1)
    extended = jnp.concatenate([samples, rim_block], axis=2)
    delayed = slice_rows(extended, station_delay, length)
    phased = polyphase(delayed, filter_taps, table, frac_delay)
    owned = width // lax.axis_size("stn")
    first_channel = lax.axis_index("stn") * owned
    channels = first_channel + jnp.arange(owned, dtype=jnp.int32)
    turned = lax.all_to_all(phased, "stn", split_axis=3, concat_axis=0, tiled=True)
    block_spectra = turned.shape[2]
    by_channel = turned.transpose(3, 0, 1, 2).reshape(owned, turned.shape[0], 2 * block_spectra)

    def one_channel(packed):
        channel, data = packed
        return detect_beams(beam_index, channel, data, width, block_spectra)

    return lax.map(one_channel, (channels, by_channel))


def solution(mesh):
    in_specs = (P("stn", None, "tm"), P(), P("stn"), P("stn"), P())
    out_specs = P("stn", None, "tm")
    return jax.shard_map(local, mesh=mesh, in_specs=in_specs, out_specs=out_specs, check_vma=False)
```

profile of v0, /device:TPU:57, one launch (start us, length us, event | category | flops | bytes accessed | tf_op | source)
XLA Modules:
  0.0 324.6 jit_solution(2123091012542506773)
XLA Ops:
  1.4 12.9 %collective-permute-start = (bf16[16,2,7296]{2,1,0:T(2,128)(2,1)S(1)}, bf16[16,2,7296]{2,1,0:T(2,128)(2,1)S(1)}, u32[]{:S(2)}, u32[]{:S(2)}) collective-permute-start(bf16[16,2,7296]{2,1,0:T(2,128)(2,1)S(1)} %slice.129), channel_id=1, source_target_pairs={{1,0},{2,1},{3,2},{4,3},{5,4},{6,5},{7,6},{8,7},{9,8},{10,9},{11,1... | collective-permute-start | bytes 1400840 | tf_op jit(solution)/shard_map/ppermute | solution.py:14
  23.6 3.7 %pad_maximum_fusion = bf16[16,2,38016]{2,1,0:T(2,128)(2,1)S(1)} fusion(bf16[16,2,7296]{2,1,0:T(2,128)(2,1)S(1)} %collective-permute-done, bf16[16,2,30720]{2,1,0:T(2,128)(2,1)} %param.7), kind=kLoop, calls=%fused_computation.29 | loop fusion | flops 4866048 | bytes 4866048 | tf_op jit(solution)/shard_map/concatenate | solution.py:85
  27.4 42.7 %while.14 = (s32[]{:T(128)}, bf16[16,2,38016]{2,1,0:T(2,128)(2,1)S(1)}, s32[16,3]{0,1:T(4,128)S(1)}, bf16[16,2,36480]{2,1,0:T(2,128)(2,1)}, s32[]{:T(128)}) while((s32[]{:T(128)}, bf16[16,2,38016]{2,1,0:T(2,128)(2,1)S(1)}, s32[16,3]{0,1:T(4,128)S(1)}, bf16[16,2,36480]{2,1,0:T(2,128)(2,1)}, s32[]{:T(128)}) %tuple.76), condition=%wide.while_cond, body=%wide.while_body.sunk | while | flops 2 | bytes 293481 | solution.py:72
  73.6 9.5 %fusion.31 = (bf16[16,2,80,384]{3,2,1,0:T(8,128)(2,1)S(1)}, bf16[16,2,80,384]{3,2,1,0:T(8,128)(2,1)S(1)}, bf16[16,2,80,384]{3,2,1,0:T(8,128)(2,1)S(1)}, bf16[16,...) fusion(bf16[16,2,95,384]{3,2,1,0:T(8,128)(2,1)S(1)} %reshape.153), kind=kLoop, calls=%fused_computation.75 | loop fusion | bytes 62914560 | tf_op jit(solution)/shard_map/slice | solution.py:38
  83.1 12.0 %fusion.22 = bf16[16,80,2,384]{3,1,0,2:T(8,128)(2,1)S(1)} fusion(f32[384]{0:T(512)S(1)} %get-tuple-element.110, bf16[16,2,80,384]{3,2,1,0:T(8,128)(2,1)} %get-tuple-element.149, f32[384]{0:T(512)S(1)} %get-tuple-element.111, bf16[16,2,80,384]{3,2,1,0:T(8,128)(2,1)S(1)} %get-tuple-element.135, f32[384]{0:T(512)S(1)} %get-tuple-element.97, ...), kind=kLoop, calls=%fused_computation.37 | loop fusion | flops 47185920 | bytes 33447936 | tf_op jit(solution)/shard_map/transpose | solution.py:42
  106.9 17.7 %all-to-all-start = ((bf16[16,2,80,384]{2,0,1,3:T(8,128)(2,1)}), bf16[16,2,80,384]{2,0,1,3:T(8,128)(2,1)S(1)}, u32[]{:S(2)}, u32[]{:S(2)}) async-start(bf16[16,2,80,384]{2,0,1,3:T(8,128)(2,1)} %copy.24), calls=%async_computation | async-start | bytes 6291456 | tf_op jit(solution)/shard_map/all_to_all | solution.py:91
  124.6 69.1 %all-to-all-done = bf16[16,2,80,384]{2,0,1,3:T(8,128)(2,1)S(1)} async-done(((bf16[16,2,80,384]{2,0,1,3:T(8,128)(2,1)}), bf16[16,2,80,384]{2,0,1,3:T(8,128)(2,1)S(1)}, u32[]{:S(2)}, u32[]{:S(2)}) %all-to-all-start) | async-done | bytes 1966112 | tf_op jit(solution)/shard_map/all_to_all | solution.py:91
  199.5 125.1 %while.13 = (s32[]{:T(128)}, f32[12,500,80]{1,2,0:T(8,128)}, s32[12]{0:T(128)S(1)}, s32[500,512]{1,0:T(8,128)S(1)}, bf16[12,512,160]{1,2,0:T(8,128)(2,1)S(1)}, /*index=5*/s32[]{:T(128)}, s32[1]{0:T(128)}) while((s32[]{:T(128)}, f32[12,500,80]{1,2,0:T(8,128)}, s32[12]{0:T(128)S(1)}, s32[500,512]{1,0:T(8,128)S(1)}, ...), condition=%wide.region_1.2_spmd, body=%wide.region_0.1_spmd.sunk | while | flops 169200000 | bytes 3836533 | solution.py:99
  200.9 4.2 %fusion.41 = f32[500,160]{0,1:T(8,128)S(1)} fusion(s32[500,512]{1,0:T(8,128)S(1)} %get-tuple-element.246, s32[]{:T(128)} %bitcast.57, bf16[12,512,160]{1,2,0:T(8,128)(2,1)S(1)} %get-tuple-element.247, s32[]{:T(128)} %get-tuple-element.236), kind=kOutput, calls=%fused_computation.7.clone.1 | convolution fusion | flops 84480000 | bytes 1516040 | tf_op jit(solution)/shard_map/while/body/eval_jaxpr/dot_general | solution.py:64
  205.1 4.1 %fusion.42 = f32[500,160]{0,1:T(8,128)S(1)} fusion(s32[500,512]{1,0:T(8,128)S(1)} %get-tuple-element.246, s32[]{:T(128)} %bitcast.57, bf16[12,512,160]{1,2,0:T(8,128)(2,1)S(1)} %get-tuple-element.247, s32[]{:T(128)} %get-tuple-element.236), kind=kOutput, calls=%fused_computation.6.clone.1 | convolution fusion | flops 84480000 | bytes 1516040 | tf_op jit(solution)/shard_map/while/body/eval_jaxpr/dot_general | solution.py:63
  211.3 4.2 %fusion.41 = f32[500,160]{0,1:T(8,128)S(1)} fusion(s32[500,512]{1,0:T(8,128)S(1)} %get-tuple-element.246, s32[]{:T(128)} %bitcast.57, bf16[12,512,160]{1,2,0:T(8,128)(2,1)S(1)} %get-tuple-element.247, s32[]{:T(128)} %get-tuple-element.236), kind=kOutput, calls=%fused_computation.7.clone.1 | convolution fusion | flops 84480000 | bytes 1516040 | tf_op jit(solution)/shard_map/while/body/eval_jaxpr/dot_general | solution.py:64
  215.5 4.1 %fusion.42 = f32[500,160]{0,1:T(8,128)S(1)} fusion(s32[500,512]{1,0:T(8,128)S(1)} %get-tuple-element.246, s32[]{:T(128)} %bitcast.57, bf16[12,512,160]{1,2,0:T(8,128)(2,1)S(1)} %get-tuple-element.247, s32[]{:T(128)} %get-tuple-element.236), kind=kOutput, calls=%fused_computation.6.clone.1 | convolution fusion | flops 84480000 | bytes 1516040 | tf_op jit(solution)/shard_map/while/body/eval_jaxpr/dot_general | solution.py:63
  221.7 4.2 %fusion.41 = f32[500,160]{0,1:T(8,128)S(1)} fusion(s32[500,512]{1,0:T(8,128)S(1)} %get-tuple-element.246, s32[]{:T(128)} %bitcast.57, bf16[12,512,160]{1,2,0:T(8,128)(2,1)S(1)} %get-tuple-element.247, s32[]{:T(128)} %get-tuple-element.236), kind=kOutput, calls=%fused_computation.7.clone.1 | convolution fusion | flops 84480000 | bytes 1516040 | tf_op jit(solution)/shard_map/while/body/eval_jaxpr/dot_general | solution.py:64
  225.9 4.1 %fusion.42 = f32[500,160]{0,1:T(8,128)S(1)} fusion(s32[500,512]{1,0:T(8,128)S(1)} %get-tuple-element.246, s32[]{:T(128)} %bitcast.57, bf16[12,512,160]{1,2,0:T(8,128)(2,1)S(1)} %get-tuple-element.247, s32[]{:T(128)} %get-tuple-element.236), kind=kOutput, calls=%fused_computation.6.clone.1 | convolution fusion | flops 84480000 | bytes 1516040 | tf_op jit(solution)/shard_map/while/body/eval_jaxpr/dot_general | solution.py:63
  232.2 4.2 %fusion.41 = f32[500,160]{0,1:T(8,128)S(1)} fusion(s32[500,512]{1,0:T(8,128)S(1)} %get-tuple-element.246, s32[]{:T(128)} %bitcast.57, bf16[12,512,160]{1,2,0:T(8,128)(2,1)S(1)} %get-tuple-element.247, s32[]{:T(128)} %get-tuple-element.236), kind=kOutput, calls=%fused_computation.7.clone.1 | convolution fusion | flops 84480000 | bytes 1516040 | tf_op jit(solution)/shard_map/while/body/eval_jaxpr/dot_general | solution.py:64
  236.3 4.1 %fusion.42 = f32[500,160]{0,1:T(8,128)S(1)} fusion(s32[500,512]{1,0:T(8,128)S(1)} %get-tuple-element.246, s32[]{:T(128)} %bitcast.57, bf16[12,512,160]{1,2,0:T(8,128)(2,1)S(1)} %get-tuple-element.247, s32[]{:T(128)} %get-tuple-element.236), kind=kOutput, calls=%fused_computation.6.clone.1 | convolution fusion | flops 84480000 | bytes 1516040 | tf_op jit(solution)/shard_map/while/body/eval_jaxpr/dot_general | solution.py:63
  242.6 4.2 %fusion.41 = f32[500,160]{0,1:T(8,128)S(1)} fusion(s32[500,512]{1,0:T(8,128)S(1)} %get-tuple-element.246, s32[]{:T(128)} %bitcast.57, bf16[12,512,160]{1,2,0:T(8,128)(2,1)S(1)} %get-tuple-element.247, s32[]{:T(128)} %get-tuple-element.236), kind=kOutput, calls=%fused_computation.7.clone.1 | convolution fusion | flops 84480000 | bytes 1516040 | tf_op jit(solution)/shard_map/while/body/eval_jaxpr/dot_general | solution.py:64
  246.8 4.1 %fusion.42 = f32[500,160]{0,1:T(8,128)S(1)} fusion(s32[500,512]{1,0:T(8,128)S(1)} %get-tuple-element.246, s32[]{:T(128)} %bitcast.57, bf16[12,512,160]{1,2,0:T(8,128)(2,1)S(1)} %get-tuple-element.247, s32[]{:T(128)} %get-tuple-element.236), kind=kOutput, calls=%fused_computation.6.clone.1 | convolution fusion | flops 84480000 | bytes 1516040 | tf_op jit(solution)/shard_map/while/body/eval_jaxpr/dot_general | solution.py:63
  253.0 4.2 %fusion.41 = f32[500,160]{0,1:T(8,128)S(1)} fusion(s32[500,512]{1,0:T(8,128)S(1)} %get-tuple-element.246, s32[]{:T(128)} %bitcast.57, bf16[12,512,160]{1,2,0:T(8,128)(2,1)S(1)} %get-tuple-element.247, s32[]{:T(128)} %get-tuple-element.236), kind=kOutput, calls=%fused_computation.7.clone.1 | convolution fusion | flops 84480000 | bytes 1516040 | tf_op jit(solution)/shard_map/while/body/eval_jaxpr/dot_general | solution.py:64
  257.2 4.1 %fusion.42 = f32[500,160]{0,1:T(8,128)S(1)} fusion(s32[500,512]{1,0:T(8,128)S(1)} %get-tuple-element.246, s32[]{:T(128)} %bitcast.57, bf16[12,512,160]{1,2,0:T(8,128)(2,1)S(1)} %get-tuple-element.247, s32[]{:T(128)} %get-tuple-element.236), kind=kOutput, calls=%fused_computation.6.clone.1 | convolution fusion | flops 84480000 | bytes 1516040 | tf_op jit(solution)/shard_map/while/body/eval_jaxpr/dot_general | solution.py:63
  263.4 4.2 %fusion.41 = f32[500,160]{0,1:T(8,128)S(1)} fusion(s32[500,512]{1,0:T(8,128)S(1)} %get-tuple-element.246, s32[]{:T(128)} %bitcast.57, bf16[12,512,160]{1,2,0:T(8,128)(2,1)S(1)} %get-tuple-element.247, s32[]{:T(128)} %get-tuple-element.236), kind=kOutput, calls=%fused_computation.7.clone.1 | convolution fusion | flops 84480000 | bytes 1516040 | tf_op jit(solution)/shard_map/while/body/eval_jaxpr/dot_general | solution.py:64
  267.6 4.1 %fusion.42 = f32[500,160]{0,1:T(8,128)S(1)} fusion(s32[500,512]{1,0:T(8,128)S(1)} %get-tuple-element.246, s32[]{:T(128)} %bitcast.57, bf16[12,512,160]{1,2,0:T(8,128)(2,1)S(1)} %get-tuple-element.247, s32[]{:T(128)} %get-tuple-element.236), kind=kOutput, calls=%fused_computation.6.clone.1 | convolution fusion | flops 84480000 | bytes 1516040 | tf_op jit(solution)/shard_map/while/body/eval_jaxpr/dot_general | solution.py:63
  273.9 4.2 %fusion.41 = f32[500,160]{0,1:T(8,128)S(1)} fusion(s32[500,512]{1,0:T(8,128)S(1)} %get-tuple-element.246, s32[]{:T(128)} %bitcast.57, bf16[12,512,160]{1,2,0:T(8,128)(2,1)S(1)} %get-tuple-element.247, s32[]{:T(128)} %get-tuple-element.236), kind=kOutput, calls=%fused_computation.7.clone.1 | convolution fusion | flops 84480000 | bytes 1516040 | tf_op jit(solution)/shard_map/while/body/eval_jaxpr/dot_general | solution.py:64
  278.0 4.1 %fusion.42 = f32[500,160]{0,1:T(8,128)S(1)} fusion(s32[500,512]{1,0:T(8,128)S(1)} %get-tuple-element.246, s32[]{:T(128)} %bitcast.57, bf16[12,512,160]{1,2,0:T(8,128)(2,1)S(1)} %get-tuple-element.247, s32[]{:T(128)} %get-tuple-element.236), kind=kOutput, calls=%fused_computation.6.clone.1 | convolution fusion | flops 84480000 | bytes 1516040 | tf_op jit(solution)/shard_map/while/body/eval_jaxpr/dot_general | solution.py:63
  284.3 4.2 %fusion.41 = f32[500,160]{0,1:T(8,128)S(1)} fusion(s32[500,512]{1,0:T(8,128)S(1)} %get-tuple-element.246, s32[]{:T(128)} %bitcast.57, bf16[12,512,160]{1,2,0:T(8,128)(2,1)S(1)} %get-tuple-element.247, s32[]{:T(128)} %get-tuple-element.236), kind=kOutput, calls=%fused_computation.7.clone.1 | convolution fusion | flops 84480000 | bytes 1516040 | tf_op jit(solution)/shard_map/while/body/eval_jaxpr/dot_general | solution.py:64
  288.5 4.1 %fusion.42 = f32[500,160]{0,1:T(8,128)S(1)} fusion(s32[500,512]{1,0:T(8,128)S(1)} %get-tuple-element.246, s32[]{:T(128)} %bitcast.57, bf16[12,512,160]{1,2,0:T(8,128)(2,1)S(1)} %get-tuple-element.247, s32[]{:T(128)} %get-tuple-element.236), kind=kOutput, calls=%fused_computation.6.clone.1 | convolution fusion | flops 84480000 | bytes 1516040 | tf_op jit(solution)/shard_map/while/body/eval_jaxpr/dot_general | solution.py:63
  294.7 4.2 %fusion.41 = f32[500,160]{0,1:T(8,128)S(1)} fusion(s32[500,512]{1,0:T(8,128)S(1)} %get-tuple-element.246, s32[]{:T(128)} %bitcast.57, bf16[12,512,160]{1,2,0:T(8,128)(2,1)S(1)} %get-tuple-element.247, s32[]{:T(128)} %get-tuple-element.236), kind=kOutput, calls=%fused_computation.7.clone.1 | convolution fusion | flops 84480000 | bytes 1516040 | tf_op jit(solution)/shard_map/while/body/eval_jaxpr/dot_general | solution.py:64
  298.9 4.1 %fusion.42 = f32[500,160]{0,1:T(8,128)S(1)} fusion(s32[500,512]{1,0:T(8,128)S(1)} %get-tuple-element.246, s32[]{:T(128)} %bitcast.57, bf16[12,512,160]{1,2,0:T(8,128)(2,1)S(1)} %get-tuple-element.247, s32[]{:T(128)} %get-tuple-element.236), kind=kOutput, calls=%fused_computation.6.clone.1 | convolution fusion | flops 84480000 | bytes 1516040 | tf_op jit(solution)/shard_map/while/body/eval_jaxpr/dot_general | solution.py:63
  305.1 4.2 %fusion.41 = f32[500,160]{0,1:T(8,128)S(1)} fusion(s32[500,512]{1,0:T(8,128)S(1)} %get-tuple-element.246, s32[]{:T(128)} %bitcast.57, bf16[12,512,160]{1,2,0:T(8,128)(2,1)S(1)} %get-tuple-element.247, s32[]{:T(128)} %get-tuple-element.236), kind=kOutput, calls=%fused_computation.7.clone.1 | convolution fusion | flops 84480000 | bytes 1516040 | tf_op jit(solution)/shard_map/while/body/eval_jaxpr/dot_general | solution.py:64
  309.3 4.1 %fusion.42 = f32[500,160]{0,1:T(8,128)S(1)} fusion(s32[500,512]{1,0:T(8,128)S(1)} %get-tuple-element.246, s32[]{:T(128)} %bitcast.57, bf16[12,512,160]{1,2,0:T(8,128)(2,1)S(1)} %get-tuple-element.247, s32[]{:T(128)} %get-tuple-element.236), kind=kOutput, calls=%fused_computation.6.clone.1 | convolution fusion | flops 84480000 | bytes 1516040 | tf_op jit(solution)/shard_map/while/body/eval_jaxpr/dot_general | solution.py:63
  315.6 4.2 %fusion.41 = f32[500,160]{0,1:T(8,128)S(1)} fusion(s32[500,512]{1,0:T(8,128)S(1)} %get-tuple-element.246, s32[]{:T(128)} %bitcast.57, bf16[12,512,160]{1,2,0:T(8,128)(2,1)S(1)} %get-tuple-element.247, s32[]{:T(128)} %get-tuple-element.236), kind=kOutput, calls=%fused_computation.7.clone.1 | convolution fusion | flops 84480000 | bytes 1516040 | tf_op jit(solution)/shard_map/while/body/eval_jaxpr/dot_general | solution.py:64
  319.7 4.1 %fusion.42 = f32[500,160]{0,1:T(8,128)S(1)} fusion(s32[500,512]{1,0:T(8,128)S(1)} %get-tuple-element.246, s32[]{:T(128)} %bitcast.57, bf16[12,512,160]{1,2,0:T(8,128)(2,1)S(1)} %get-tuple-element.247, s32[]{:T(128)} %get-tuple-element.236), kind=kOutput, calls=%fused_computation.6.clone.1 | convolution fusion | flops 84480000 | bytes 1516040 | tf_op jit(solution)/shard_map/while/body/eval_jaxpr/dot_general | solution.py:63
  (102 shorter events, 91.0 us)
Async XLA Ops:
  0.0 22.2 %copy-start.2 = (f32[16]{0:T(128)S(1)}, f32[16]{0:T(128)}, u32[]{:S(2)}) copy-start(f32[16]{0:T(128)} %param.9) | copy-start | bytes 196
  1.4 22.3 %collective-permute-start = (bf16[16,2,7296]{2,1,0:T(2,128)(2,1)S(1)}, bf16[16,2,7296]{2,1,0:T(2,128)(2,1)S(1)}, u32[]{:S(2)}, u32[]{:S(2)}) collective-permute-start(bf16[16,2,7296]{2,1,0:T(2,128)(2,1)S(1)} %slice.129), channel_id=1, source_target_pairs={{1,0},{2,1},{3,2},{4,3},{5,4},{6,5},{7,6},{8,7},{9,8},{10,9},{11,1... | collective-permute-start | bytes 1400840 | tf_op jit(solution)/shard_map/ppermute | solution.py:14
  97.1 2.2 copy-start
  106.9 86.8 %all-to-all-start = ((bf16[16,2,80,384]{2,0,1,3:T(8,128)(2,1)}), bf16[16,2,80,384]{2,0,1,3:T(8,128)(2,1)S(1)}, u32[]{:S(2)}, u32[]{:S(2)}) async-start(bf16[16,2,80,384]{2,0,1,3:T(8,128)(2,1)} %copy.24), calls=%async_computation | async-start | bytes 6291456 | tf_op jit(solution)/shard_map/all_to_all | solution.py:91
  196.2 3.3 %copy-start.1 = (s32[500,512]{1,0:T(8,128)S(1)}, s32[500,512]{1,0:T(8,128)}, u32[]{:S(2)}) copy-start(s32[500,512]{1,0:T(8,128)} %param.11) | copy-start | bytes 3072004
where the time goes:
time: 326 us; the launch traced here: 325 us
  matrix products  103 us (32%)
  local copies, waits for them, and re-layouts  79.5 us (24%)
  waiting for transfers between devices  70.3 us (22%)
  other arithmetic  32.3 us (10%)
  starting transfers between devices  30.6 us (9%)
  loops' own time  8.58 us (3%)
    all_to_all x1, waiting for transfers between devices, local(): lax.all_to_all(phased, 'stn', split_axis=3, concat_axis=0, tiled=True)  69.1 us
    dot_general x12, matrix products, detect_beams(): second = jnp.dot(weight_im, data, preferred_element_type=jnp.float32)  50.2 us
    dot_general x12, matrix products, detect_beams(): first = jnp.dot(weight_re, data, preferred_element_type=jnp.float32)  49.7 us
    gather x48, local copies, waits for them, and re-layouts  42.7 us
    all_to_all x1, starting transfers between devices, local(): lax.all_to_all(phased, 'stn', split_axis=3, concat_axis=0, tiled=True)  17.7 us
    ppermute x1, starting transfers between devices, from_behind(): lax.ppermute(value, axis, [(source, source + steps) for source in range(i...  12.9 us
    transpose x1, other arithmetic, polyphase(): summed.astype(jnp.bfloat16).transpose(0, 2, 1, 3)  12 us
    slice x1, local copies, waits for them, and re-layouts, polyphase(): blocks[:, :, tap_index:tap_index + spectra, :].astype(jnp.float32)  9.52 us
  transfers between devices with their start and end apart: 2, of which 2 were waited for; matrix products, arithmetic and copies ran while one was open for 2% of the time, Pallas kernels for 0%

commit v1 on v0

v1 whole, which is shorter than its diff:
```python
import functools
import math

import jax
import jax.numpy as jnp
import ml_dtypes
import numpy as np
from jax import lax
from jax.experimental import pallas as pl
from jax.experimental.pallas import tpu as pltpu
from jax.sharding import PartitionSpec as P

TAPS = 16
C = 384
B = 500
LANES = 128
COLS = C // LANES
DSPEC = 4
STN = 32
ST = 16
KS = 80
KG = KS // 16
GROUPS = 3
CPG = 4
REACH = (TAPS - 1 + DSPEC) * C
SPAN = KS * C
DCOLS = (KS + TAPS - 1) * COLS
MESH = pl.DeviceIdType.MESH


def sincos_turns(r):
    h = r * math.pi
    z = h * h
    s = jnp.full_like(r, 1.0 / 6227020800.0)
    for c in (-1.0 / 39916800.0, 1.0 / 362880.0, -1.0 / 5040.0, 1.0 / 120.0, -1.0 / 6.0, 1.0):
        s = s * z + c
    s = s * h
    q = jnp.full_like(r, 1.0 / 479001600.0)
    for c in (-1.0 / 3628800.0, 1.0 / 40320.0, -1.0 / 720.0, 1.0 / 24.0, -0.5, 1.0):
        q = q * z + c
    return 1.0 - 2.0 * s * s, 2.0 * s * q


def column_channels():
    lane = np.arange(LANES)
    dest, sub = lane % STN, lane // STN
    own = C // STN
    return np.stack([dest * own + g * CPG + sub for g in range(GROUPS)])


def dft_columns():
    chan = column_channels()
    n = np.arange(C)
    parts = []
    for g in range(GROUPS):
        angle = 2.0 * np.pi / C * ((n[:, None] * chan[g][None, :]) % C)
        cosine = np.cos(angle) / math.sqrt(C)
        sine = np.sin(angle) / math.sqrt(C)
        upper = np.concatenate([cosine, -sine], axis=1)
        lower = np.concatenate([sine, cosine], axis=1)
        parts.append(np.concatenate([upper, lower], axis=0))
    return np.stack(parts).astype(ml_dtypes.bfloat16)


def polyphase_kernel(main_ref, halo_ref, delay_ref, taps_ref, f_ref, ext, dly):
    delay = jnp.broadcast_to(delay_ref[...], (ST, LANES))
    lane = lax.broadcasted_iota(jnp.int32, (ST, LANES), 1)
    rest = delay & (LANES - 1)
    index = (lane + rest) & (LANES - 1)
    keep = lane < LANES - rest
    bits = [(delay & (LANES << b)) != 0 for b in range(4)]
    total = (SPAN + REACH) // LANES
    for r in range(2):
        ext[r, :, :SPAN] = main_ref[r].astype(jnp.float32)
        ext[r, :, SPAN:] = halo_ref[r].astype(jnp.float32)

    chunk = 15

    def align(step, _):
        base = step * chunk
        for r in range(2):
            cols = []
            for j in range(chunk + 16):
                at = pl.multiple_of(jnp.minimum(base + j, total - 1) * LANES, LANES)
                cols.append(ext[r, :, pl.ds(at, LANES)])
            for b in (3, 2, 1, 0):
                cols = [jnp.where(bits[b], cols[j + (1 << b)], cols[j]) for j in range(len(cols) - (1 << b))]
            turned = [
                jnp.take_along_axis(col, index, axis=1, mode="promise_in_bounds")
                for col in cols[: chunk + 1]
            ]
            for j in range(chunk):
                at = pl.multiple_of((base + j) * LANES, LANES)
                dly[r, :, pl.ds(at, LANES)] = jnp.where(keep, turned[j], turned[j + 1])
        return 0

    lax.fori_loop(0, DCOLS // chunk, align, 0)

    per = 8

    def filt(step, _):
        for r in range(2):
            for m in range(COLS):
                sums = [None] * per
                for j in range(per + TAPS - 1):
                    at = pl.multiple_of((step * per + j) * C + m * LANES, LANES)
                    col = dly[r, :, pl.ds(at, LANES)]
                    for i in range(max(0, j - TAPS + 1), min(per, j + 1)):
                        p = j - i
                        term = col * taps_ref[p : p + 1, m * LANES : (m + 1) * LANES]
                        sums[i] = term if sums[i] is None else sums[i] + term
                for i in range(per):
                    row = pl.multiple_of((step * per + i) * ST, ST)
                    f_ref[pl.ds(row, ST), r * C + m * LANES : r * C + (m + 1) * LANES] = sums[i].astype(jnp.bfloat16)
        return 0

    lax.fori_loop(0, KS // per, filt, 0)


def polyphase(main, halo, delay, taps):
    vmem = pl.BlockSpec(memory_space=pltpu.VMEM)
    return pl.pallas_call(
        polyphase_kernel,
        out_shape=jax.ShapeDtypeStruct((KS * ST, 2 * C), jnp.bfloat16),
        in_specs=[vmem] * 4,
        out_specs=vmem,
        scratch_shapes=[
            pltpu.VMEM((2, ST, SPAN + REACH), jnp.float32),
            pltpu.VMEM((2, ST, DCOLS * LANES), jnp.float32),
        ],
        compiler_params=pltpu.CompilerParams(vmem_limit_bytes=40 << 20),
    )(main, halo, delay, taps)


def butterfly(vregs, lane, widths):
    vregs = list(vregs)
    for j, w in enumerate(widths):
        mask = (lane & w) != 0
        out = list(vregs)
        for i in range(len(vregs)):
            if not i & (1 << j):
                k = i | (1 << j)
                out[i] = jnp.where(mask, pltpu.roll(vregs[k], w, 1), vregs[i])
                out[k] = jnp.where(mask, vregs[k], pltpu.roll(vregs[i], LANES - w, 1))
        vregs = out
    return vregs


def beam_kernel(f_ref, table_ref, offset_ref, frac_ref, index_ref, out_ref, msg, recv, weights, rhs, send_sem, recv_sem, own_sem):
    me = lax.axis_index("stn")
    barrier = pltpu.get_barrier_semaphore()

    def greet(i, _):
        pl.semaphore_signal(barrier, inc=1, device_id={"stn": lax.rem(me + i, STN)}, device_id_type=MESH)
        return 0

    lax.fori_loop(1, STN, greet, 0)
    lane = lax.broadcasted_iota(jnp.int32, (ST, LANES), 1)

    for g in range(GROUPS):
        phase = frac_ref[...] * offset_ref[g : g + 1, :]
        cosine, sine = sincos_turns(phase)

        def spectra(kg, _):
            rows = pl.ds(pl.multiple_of(kg * 256, 256), 256)
            spec = jnp.dot(f_ref[rows, :], table_ref[g], preferred_element_type=jnp.float32)
            turned = [[], []]
            for k in range(16):
                re = spec[k * ST : (k + 1) * ST, :LANES]
                im = spec[k * ST : (k + 1) * ST, LANES:]
                turned[0].append((re * cosine - im * sine).astype(jnp.bfloat16))
                turned[1].append((re * sine + im * cosine).astype(jnp.bfloat16))
            blocks = butterfly(turned[0] + turned[1], lane, (1, 2, 4, 8, 16))
            for d in range(STN):
                msg[g, d, kg] = blocks[d]
            return 0

        lax.fori_loop(0, KG, spectra, 0)
        if g == 0:
            pl.semaphore_wait(barrier, STN - 1)

        def post(i, _):
            to = lax.rem(me + i, STN)
            pltpu.make_async_remote_copy(
                src_ref=msg.at[g, to],
                dst_ref=recv.at[g, me],
                send_sem=send_sem.at[g],
                recv_sem=recv_sem.at[g],
                device_id={"stn": to},
                device_id_type=MESH,
            ).start()
            return 0

        lax.fori_loop(1, STN, post, 0)
        pltpu.make_async_copy(msg.at[g, me], recv.at[g, me], own_sem.at[g]).start()

    own = C // STN
    first = (me * own - C // 2).astype(jnp.float32)

    def weigh(at, rows):
        index = index_ref[pl.ds(at, rows), :].astype(jnp.float32)
        step = index * (1.0 / (16 * C))
        start = index * first * (1.0 / (16 * C))
        step_re, step_im = sincos_turns(step)
        now_re, now_im = sincos_turns(start - jnp.round(start))
        for c in range(own):
            weights[c, pl.ds(at, rows), :512] = now_re.astype(jnp.bfloat16)
            weights[c, pl.ds(at, rows), 512:] = now_im.astype(jnp.bfloat16)
            if c < own - 1:
                now_re, now_im = now_re * step_re - now_im * step_im, now_re * step_im + now_im * step_re

    def weigh_step(i, _):
        weigh(pl.multiple_of(i * 16, 16), 16)
        return 0

    lax.fori_loop(0, 512 // 16, weigh_step, 0)

    zero = jnp.zeros((ST, LANES), jnp.bfloat16)
    for g in range(GROUPS):
        pltpu.make_async_copy(msg.at[g, 0 : STN - 1], recv.at[g, 0 : STN - 1], recv_sem.at[g]).wait()
        pltpu.make_async_copy(msg.at[g, me], recv.at[g, me], own_sem.at[g]).wait()

        def unpack(e, _):
            blocks = [recv[g, e, kg] for kg in range(KG)] + [zero] * (8 - KG)
            blocks = butterfly(blocks, lane, (16, 32, 64))
            upper = pl.ds(pl.multiple_of(e * ST, ST), ST)
            lower = pl.ds(pl.multiple_of(512 + e * ST, ST), ST)
            for c in range(CPG):
                re, im = blocks[2 * c], blocks[2 * c + 1]
                rhs[c, upper, :LANES] = re
                rhs[c, upper, LANES:] = im
                rhs[c, lower, :LANES] = -im
                rhs[c, lower, LANES:] = re
            return 0

        lax.fori_loop(0, STN, unpack, 0)

        def detect(c, _):
            beam = jnp.dot(weights[g * CPG + c], rhs[c], preferred_element_type=jnp.float32)
            re = beam[:, :LANES]
            im = beam[:, LANES:]
            power = (re * re + im * im) * (1.0 / 512)
            out_ref[g * CPG + c] = power[:B, :KS]
            return 0

        lax.fori_loop(0, CPG, detect, 0)

    for g in range(GROUPS):
        pltpu.make_async_copy(msg.at[g, 0 : STN - 1], recv.at[g, 0 : STN - 1], send_sem.at[g]).wait()


def beams(f, table, offset, frac, index):
    vmem = pl.BlockSpec(memory_space=pltpu.VMEM)
    own = C // STN
    return pl.pallas_call(
        beam_kernel,
        out_shape=jax.ShapeDtypeStruct((own, B, KS), jnp.float32),
        in_specs=[vmem] * 5,
        out_specs=vmem,
        scratch_shapes=[
            pltpu.VMEM((GROUPS, STN, KG, ST, LANES), jnp.bfloat16),
            pltpu.VMEM((GROUPS, STN, KG, ST, LANES), jnp.bfloat16),
            pltpu.VMEM((own, 512, 1024), jnp.bfloat16),
            pltpu.VMEM((CPG, 1024, 2 * LANES), jnp.bfloat16),
            pltpu.SemaphoreType.DMA((GROUPS,)),
            pltpu.SemaphoreType.DMA((GROUPS,)),
            pltpu.SemaphoreType.DMA((GROUPS,)),
        ],
        compiler_params=pltpu.CompilerParams(collective_id=0, has_side_effects=True, vmem_limit_bytes=56 << 20),
    )(f, table, offset, frac, index)


def local(samples, filter_taps, frac_delay, station_delay, beam_index):
    count = lax.axis_size("tm")
    head = samples[:, :, :REACH]
    halo = lax.ppermute(head, "tm", [(i, i - 1) for i in range(1, count)])
    main = samples.transpose(1, 0, 2)
    halo = halo.transpose(1, 0, 2)
    f = polyphase(main, halo, station_delay[:, None], filter_taps)
    table = jnp.asarray(dft_columns())
    offset = jnp.asarray((column_channels() - C // 2).astype(np.float32) / C)
    index = jnp.pad(beam_index, ((0, 512 - B), (0, 0)))
    return beams(f, table, offset, frac_delay[:, None], index)


def solution(mesh):
    in_specs = (P("stn", None, "tm"), P(), P("stn"), P("stn"), P())
    out_specs = P("stn", None, "tm")
    return jax.shard_map(local, mesh=mesh, in_specs=in_specs, out_specs=out_specs, check_vma=False)
```

time: 326 us -> 113 us (0.35)
  matrix products: 103 us -> 0 us
  Pallas kernels: 0 us -> 82.9 us
  local copies, waits for them, and re-layouts: 79.5 us -> 10.6 us
  waiting for transfers between devices: 70.3 us -> 5.7 us
  other arithmetic: 32.3 us -> 0 us
  starting transfers between devices: 30.6 us -> 13 us
  loops' own time: 8.58 us -> 0 us
    dot_general x25 -> x0, matrix products: 103 us -> none  [the longest x12 50.2 us: detect_beams(): second = jnp.dot(weight_im, data, preferred_element_type=jnp.float32)]
    pallas_call x0 -> x2, Pallas kernels: none -> 82.9 us  [the longest x1 74.5 us: beams(): pl.pallas_call(beam_kernel, out_shape=jax.ShapeDtypeStruct((own, B, KS),...]
    all_to_all x1 -> x0, waiting for transfers between devices: 69.1 us -> none  [local(): lax.all_to_all(phased, 'stn', split_axis=3, concat_axis=0, tiled=True)]
    gather x48 -> x0, local copies, waits for them, and re-layouts: 42.7 us -> none
    all_to_all x1 -> x0, starting transfers between devices: 17.7 us -> none  [local(): lax.all_to_all(phased, 'stn', split_axis=3, concat_axis=0, tiled=True)]
    transpose x1 -> x0, other arithmetic: 12 us -> none  [polyphase(): summed.astype(jnp.bfloat16).transpose(0, 2, 1, 3)]
    slice x3 -> x1, local copies, waits for them, and re-layouts: 12 us -> 1.34 us  [local(): head = samples[:, :, :REACH]]
    dynamic_update_slice x12 -> x0, other arithmetic: 8.7 us -> none  [local(): return lax.map(one_channel, (channels, by_channel))]
  transfers between devices with their start and end apart: 2 -> 1, of which waited for: 2 -> 1; matrix products, arithmetic and copies ran while one was open for 2% -> 3% of each run, Pallas kernels for 0% -> 0%
where the time goes in v1:
time: 113 us; the launch traced here: 112 us
  Pallas kernels  82.9 us (73%)
  starting transfers between devices  13 us (12%)
  local copies, waits for them, and re-layouts  10.6 us (9%)
  waiting for transfers between devices  5.7 us (5%)
    pallas_call x1, Pallas kernels, beams(): pl.pallas_call(beam_kernel, out_shape=jax.ShapeDtypeStruct((own, B, KS),...  74.5 us
    ppermute x1, starting transfers between devices, local(): halo = lax.ppermute(head, 'tm', [(i, i - 1) for i in range(1, count)])  13 us
    pallas_call x1, Pallas kernels, polyphase(): pl.pallas_call(polyphase_kernel, out_shape=jax.ShapeDtypeStruct((KS * ST,...  8.43 us
    ppermute x1, waiting for transfers between devices, local(): halo = lax.ppermute(head, 'tm', [(i, i - 1) for i in range(1, count)])  5.7 us
    unnamed x12, local copies, waits for them, and re-layouts  4.22 us
    pallas_call x1, local copies, waits for them, and re-layouts, beams(): pl.pallas_call(beam_kernel, out_shape=jax.ShapeDtypeStruct((own, B, KS),...  3.28 us
  transfers between devices with their start and end apart: 1, of which 1 were waited for; matrix products, arithmetic and copies ran while one was open for 3% of the time, Pallas kernels for 0%

profile of v1, /device:TPU:57, one launch (start us, length us, event | category | flops | bytes accessed | tf_op | source)
XLA Modules:
  0.0 112.4 jit_solution(6283422428778222903)
XLA Ops:
  0.0 1.3 %slice.4 = bf16[16,2,7296]{2,1,0:T(2,128)(2,1)S(1)} slice(bf16[16,2,30720]{2,1,0:T(2,128)(2,1)} %param.7), slice={[0:16], [0:2], [0:7296]} | slice | bytes 933888 | tf_op jit(solution)/shard_map/slice | solution.py:275
  1.3 0.8 copy.14
  2.2 0.0 copy-start.3
  2.2 0.0 copy-start.4
  2.2 0.0 copy-start.2
  2.2 13.0 %collective-permute-start = (bf16[16,2,7296]{2,0,1:T(8,128)(2,1)}, bf16[16,2,7296]{2,0,1:T(8,128)(2,1)S(1)}, u32[]{:S(2)}, u32[]{:S(2)}) collective-permute-start(bf16[16,2,7296]{2,0,1:T(8,128)(2,1)} %copy.14), channel_id=1, source_target_pairs={{1,0},{2,1},{3,2},{4,3},{5,4},{6,5},{7,6},{8,7},{9,8},{10,9},{11,1... | collective-permute-start | bytes 1400840 | tf_op jit(solution)/shard_map/ppermute | solution.py:276
  15.2 2.1 %copy.15 = bf16[16,2,30720]{2,0,1:T(8,128)(2,1)S(1)} copy(bf16[16,2,30720]{2,1,0:T(2,128)(2,1)} %param.7) | data formatting | bytes 3932160 | tf_op args[0]
  17.3 0.0 copy-start.1
  17.3 0.0 copy-done.3
  17.4 0.7 copy.11.frac_ref
  18.0 0.0 copy-done.4
  18.0 0.1 copy.10.delay_ref
  18.1 0.0 copy-done.2
  18.1 1.0 pad.4.index_ref
  19.2 5.7 %collective-permute-done = bf16[16,2,7296]{2,0,1:T(8,128)(2,1)S(1)} collective-permute-done((bf16[16,2,7296]{2,0,1:T(8,128)(2,1)}, bf16[16,2,7296]{2,0,1:T(8,128)(2,1)S(1)}, u32[]{:S(2)}, u32[]{:S(2)}) %collective-permute-start) | collective-permute-done | bytes 466976 | tf_op jit(solution)/shard_map/ppermute | solution.py:276
  24.9 0.0 copy-done.1
  24.9 8.4 %shard_map.73.f_ref = bf16[1280,768]{1,0:T(8,128)(2,1)S(1)} custom-call(bf16[2,16,30720]{2,1,0:T(8,128)(2,1)S(1)} %bitcast.6, bf16[2,16,7296]{2,1,0:T(8,128)(2,1)S(1)} %bitcast.7, s32[16,1]{1,0:T(8,128)S(1)} %copy.10.delay_ref, f32[16,384]{1,0:T(8,128)S(1)} %copy-done.1), custom_call_target="tpu_custom_call" | custom-call | tf_op jit(solution)/shard_map/pallas_call | solution.py:122
  33.3 0.0 copy-start
  33.3 1.3 %copy-done = bf16[1280,768]{1,0:T(8,128)(2,1)} copy-done((bf16[1280,768]{1,0:T(8,128)(2,1)}, bf16[1280,768]{1,0:T(8,128)(2,1)S(1)}, u32[]{:S(2)}) %copy-start) | copy-done | bytes 1966104
  34.6 74.5 %shard_map.74 = f32[12,500,80]{2,1,0:T(8,128)} custom-call(bf16[1280,768]{1,0:T(8,128)(2,1)} %copy-done, bf16[3,768,256]{2,1,0:T(8,128)(2,1)} %constant.6.clone.table_ref, f32[3,128]{1,0:T(4,128)} %constant.7.clone.offset_ref, f32[16,1]{1,0:T(8,128)} %copy.11.frac_ref, s32[512,512]{1,0:T(8,128)} %pad.4.index_ref), custom_call_target="tpu_custom_call" | custom-call | tf_op jit(solution)/shard_map/pallas_call | solution.py:255
  109.1 3.3 %copy.12 = f32[12,500,80]{1,2,0:T(8,128)} copy(f32[12,500,80]{2,1,0:T(8,128)} %shard_map.74) | data formatting | bytes 3840000 | tf_op jit(solution)/shard_map/pallas_call | solution.py:255
Async XLA Ops:
  2.2 15.2 %copy-start.3 = (f32[16]{0:T(128)S(1)}, f32[16]{0:T(128)}, u32[]{:S(2)}) copy-start(f32[16]{0:T(128)} %param.9) | copy-start | bytes 196
  2.2 15.9 %copy-start.4 = (s32[16]{0:T(128)S(1)}, s32[16]{0:T(128)}, u32[]{:S(2)}) copy-start(s32[16]{0:T(128)} %param.10) | copy-start | bytes 196
  2.2 15.9 %copy-start.2 = (s32[500,512]{1,0:T(8,128)S(1)}, s32[500,512]{1,0:T(8,128)}, u32[]{:S(2)}) copy-start(s32[500,512]{1,0:T(8,128)} %param.11) | copy-start | bytes 3072004
  2.2 22.7 %collective-permute-start = (bf16[16,2,7296]{2,0,1:T(8,128)(2,1)}, bf16[16,2,7296]{2,0,1:T(8,128)(2,1)S(1)}, u32[]{:S(2)}, u32[]{:S(2)}) collective-permute-start(bf16[16,2,7296]{2,0,1:T(8,128)(2,1)} %copy.14), channel_id=1, source_target_pairs={{1,0},{2,1},{3,2},{4,3},{5,4},{6,5},{7,6},{8,7},{9,8},{10,9},{11,1... | collective-permute-start | bytes 1400840 | tf_op jit(solution)/shard_map/ppermute | solution.py:276
  17.3 7.5 %copy-start.1 = (f32[16,384]{1,0:T(8,128)S(1)}, f32[16,384]{1,0:T(8,128)}, u32[]{:S(2)}) copy-start(f32[16,384]{1,0:T(8,128)} %taps_ref.1) | copy-start | bytes 73732
  33.3 1.3 %copy-start = (bf16[1280,768]{1,0:T(8,128)(2,1)}, bf16[1280,768]{1,0:T(8,128)(2,1)S(1)}, u32[]{:S(2)}) copy-start(bf16[1280,768]{1,0:T(8,128)(2,1)S(1)} %shard_map.73.f_ref) | copy-start | bytes 5898244

commit v2 on v1

v2 whole, which is shorter than its diff:
```python
import math

import jax
import jax.numpy as jnp
import ml_dtypes
import numpy as np
from jax import lax
from jax.experimental import pallas as pl
from jax.experimental.pallas import tpu as pltpu
from jax.sharding import PartitionSpec as P

TAPS = 16
C = 384
B = 500
LANES = 128
COLS = C // LANES
DSPEC = 4
STN = 32
ST = 16
KS = 80
KG = KS // 16
GROUPS = 3
CPG = 4
REACH = (TAPS - 1 + DSPEC) * C
SPAN = KS * C
DCOLS = (KS + TAPS - 1) * COLS
PHASES = ((0, 1), (1, 3), (3, 5))
CHUNK = 24
RIM = (TAPS - 1) * COLS + 48 * PHASES[-1][0]
RIM_COLS = SPAN // LANES - RIM
EXT_COLS = DCOLS + 16 - RIM
MESH = pl.DeviceIdType.MESH


def sincos_turns(r):
    h = r * math.pi
    z = h * h
    s = jnp.full_like(r, 1.0 / 6227020800.0)
    for c in (-1.0 / 39916800.0, 1.0 / 362880.0, -1.0 / 5040.0, 1.0 / 120.0, -1.0 / 6.0, 1.0):
        s = s * z + c
    s = s * h
    q = jnp.full_like(r, 1.0 / 479001600.0)
    for c in (-1.0 / 3628800.0, 1.0 / 40320.0, -1.0 / 720.0, 1.0 / 24.0, -0.5, 1.0):
        q = q * z + c
    return 1.0 - 2.0 * s * s, 2.0 * s * q


def column_channels():
    lane = np.arange(LANES)
    dest, sub = lane % STN, lane // STN
    own = C // STN
    return np.stack([dest * own + g * CPG + sub for g in range(GROUPS)])


def dft_columns():
    chan = column_channels()
    n = np.arange(C)
    parts = []
    for g in range(GROUPS):
        angle = 2.0 * np.pi / C * ((n[:, None] * chan[g][None, :]) % C)
        cosine = np.cos(angle) / math.sqrt(C)
        sine = np.sin(angle) / math.sqrt(C)
        upper = np.concatenate([cosine, -sine], axis=1)
        lower = np.concatenate([sine, cosine], axis=1)
        parts.append(np.concatenate([upper, lower], axis=0))
    return np.stack(parts).astype(ml_dtypes.bfloat16)


def butterfly(vregs, lane, widths):
    vregs = list(vregs)
    for j, w in enumerate(widths):
        mask = (lane & w) != 0
        out = list(vregs)
        for i in range(len(vregs)):
            if not i & (1 << j):
                k = i | (1 << j)
                out[i] = jnp.where(mask, pltpu.roll(vregs[k], w, 1), vregs[i])
                out[k] = jnp.where(mask, vregs[k], pltpu.roll(vregs[i], LANES - w, 1))
        vregs = out
    return vregs


def station_rows(values_ref):
    row = lax.broadcasted_iota(jnp.int32, (ST, LANES), 0)
    out = jnp.full((ST, LANES), values_ref[0])
    for i in range(1, ST):
        out = jnp.where(row == i, values_ref[i], out)
    return out


def kernel(main_ref, delay_ref, frac_ref, taps_ref, table_ref, offset_ref, index_ref, out_ref, ext, dly, frames, msg, recv, weights, rhs, power, send_sem, recv_sem, own_sem, halo_sem, out_sem):
    me = lax.axis_index("stn")
    tm = lax.axis_index("tm")
    count = lax.axis_size("tm")
    barrier = pltpu.get_barrier_semaphore()

    def greet(i, _):
        pl.semaphore_signal(barrier, inc=1, device_id={"stn": lax.rem(me + i, STN)}, device_id_type=MESH)
        return 0

    lax.fori_loop(1, STN, greet, 0)
    pl.semaphore_signal(barrier, inc=1, device_id={"tm": lax.rem(tm + 1, count)}, device_id_type=MESH)

    delay = station_rows(delay_ref)
    frac = station_rows(frac_ref)
    lane = lax.broadcasted_iota(jnp.int32, (ST, LANES), 1)
    rest = delay & (LANES - 1)
    index = (lane + rest) & (LANES - 1)
    keep = lane < LANES - rest
    bits = [(delay & (LANES << b)) != 0 for b in range(4)]

    ext[:, :, : RIM_COLS * LANES] = main_ref[:, :, RIM * LANES :]
    ext[:, :, RIM_COLS * LANES + REACH :] = jnp.zeros((2, ST, EXT_COLS * LANES - RIM_COLS * LANES - REACH), jnp.bfloat16)

    pl.semaphore_wait(barrier, STN)

    def halo(to):
        return pltpu.make_async_remote_copy(
            src_ref=main_ref.at[:, :, :REACH],
            dst_ref=ext.at[:, :, RIM_COLS * LANES : RIM_COLS * LANES + REACH],
            send_sem=halo_sem.at[0],
            recv_sem=halo_sem.at[1],
            device_id={"tm": to},
            device_id_type=MESH,
        )

    @pl.when(tm > 0)
    def _():
        halo(tm - 1).start()

    @pl.when(tm == count - 1)
    def _():
        ext[:, :, RIM_COLS * LANES : RIM_COLS * LANES + REACH] = jnp.zeros((2, ST, REACH), jnp.bfloat16)

    def align(source, base, shift):
        for r in range(2):
            cols = []
            for j in range(CHUNK + 16):
                at = pl.multiple_of((base + j - shift) * LANES, LANES)
                cols.append(source[r, :, pl.ds(at, LANES)])
            for b in (3, 2, 1, 0):
                cols = [jnp.where(bits[b], cols[j + (1 << b)], cols[j]) for j in range(len(cols) - (1 << b))]
            turned = [
                jnp.take_along_axis(col.astype(jnp.float32), index, axis=1, mode="promise_in_bounds")
                for col in cols[: CHUNK + 1]
            ]
            for j in range(CHUNK):
                at = pl.multiple_of((base + j) * LANES, LANES)
                dly[r, :, pl.ds(at, LANES)] = jnp.where(keep, turned[j], turned[j + 1])

    per = 8

    def filt(step):
        for r in range(2):
            for m in range(COLS):
                sums = [None] * per
                for j in range(per + TAPS - 1):
                    at = pl.multiple_of((step * per + j) * C + m * LANES, LANES)
                    col = dly[r, :, pl.ds(at, LANES)]
                    for i in range(max(0, j - TAPS + 1), min(per, j + 1)):
                        p = j - i
                        term = col * taps_ref[p : p + 1, m * LANES : (m + 1) * LANES]
                        sums[i] = term if sums[i] is None else sums[i] + term
                for i in range(per):
                    row = pl.multiple_of((step * per + i) * ST, ST)
                    frames[pl.ds(row, ST), r * C + m * LANES : r * C + (m + 1) * LANES] = sums[i].astype(jnp.bfloat16)

    def spectra(g, kg, cosine, sine):
        spec = jnp.dot(frames[kg * 256 : (kg + 1) * 256, :], table_ref[g], preferred_element_type=jnp.float32)
        turned = [[], []]
        for k in range(16):
            re = spec[k * ST : (k + 1) * ST, :LANES]
            im = spec[k * ST : (k + 1) * ST, LANES:]
            turned[0].append((re * cosine - im * sine).astype(jnp.bfloat16))
            turned[1].append((re * sine + im * cosine).astype(jnp.bfloat16))
        blocks = butterfly(turned[0] + turned[1], lane, (1, 2, 4, 8, 16))
        for d in range(STN):
            msg[g, d, kg] = blocks[d]

    def loop(start, stop, step):
        def body(i, _):
            step(i)
            return 0

        lax.fori_loop(start, stop, body, 0)

    loop(0, 48 // CHUNK, lambda i: align(main_ref, i * CHUNK, 0))
    for number, (begin, end) in enumerate(PHASES):
        last = number == len(PHASES) - 1
        if last:
            @pl.when(tm < count - 1)
            def _():
                halo(tm).wait_recv()

        source, shift = (ext, RIM) if last else (main_ref, 0)
        first_col = (TAPS - 1) * COLS + 48 * begin
        loop(0, (end - begin) * 48 // CHUNK, lambda i: align(source, first_col + i * CHUNK, shift))
        loop(begin * 16 // per, end * 16 // per, filt)
        for g in range(GROUPS):
            cosine, sine = sincos_turns(frac * offset_ref[g : g + 1, :])
            for kg in range(begin, end):
                spectra(g, kg, cosine, sine)

            def post(i, _):
                to = lax.rem(me + i, STN)
                pltpu.make_async_remote_copy(
                    src_ref=msg.at[g, to, begin:end],
                    dst_ref=recv.at[g, me, begin:end],
                    send_sem=send_sem.at[g],
                    recv_sem=recv_sem.at[g],
                    device_id={"stn": to},
                    device_id_type=MESH,
                ).start()
                return 0

            lax.fori_loop(1, STN, post, 0)
            if last:
                pltpu.make_async_copy(msg.at[g, me], recv.at[g, me], own_sem.at[g]).start()

    own = C // STN
    first = (me * own - C // 2).astype(jnp.float32)

    def weigh(at, rows):
        rows = rows.astype(jnp.float32)
        step_re, step_im = sincos_turns(rows * (1.0 / (16 * C)))
        start = rows * first * (1.0 / (16 * C))
        now_re, now_im = sincos_turns(start - jnp.round(start))
        for c in range(own):
            weights[c, pl.ds(at, 16), :512] = now_re.astype(jnp.bfloat16)
            weights[c, pl.ds(at, 16), 512:] = now_im.astype(jnp.bfloat16)
            if c < own - 1:
                now_re, now_im = now_re * step_re - now_im * step_im, now_re * step_im + now_im * step_re

    def weigh_step(i):
        at = pl.multiple_of(i * 16, 16)
        weigh(at, index_ref[pl.ds(at, 16), :])

    loop(0, B // 16, weigh_step)
    tail = B // 16 * 16
    weigh(tail, jnp.concatenate([index_ref[tail:, :], jnp.zeros((16 - B % 16, 512), jnp.int32)], axis=0))

    per_step = 4
    wide = lax.broadcasted_iota(jnp.int32, (per_step * ST, LANES), 1)
    zero = jnp.zeros((per_step * ST, LANES), jnp.bfloat16)
    for g in range(GROUPS):
        pltpu.make_async_copy(msg.at[g, 0 : STN - 1], recv.at[g, 0 : STN - 1], recv_sem.at[g]).wait()
        pltpu.make_async_copy(msg.at[g, me], recv.at[g, me], own_sem.at[g]).wait()

        def unpack(e):
            blocks = [recv[g, pl.ds(e * per_step, per_step), kg].reshape(per_step * ST, LANES) for kg in range(KG)]
            blocks = butterfly(blocks + [zero] * (8 - KG), wide, (16, 32, 64))
            upper = pl.ds(pl.multiple_of(e * per_step * ST, per_step * ST), per_step * ST)
            lower = pl.ds(pl.multiple_of(512 + e * per_step * ST, per_step * ST), per_step * ST)
            for c in range(CPG):
                re, im = blocks[2 * c], blocks[2 * c + 1]
                rhs[c, upper, :LANES] = re
                rhs[c, upper, LANES:] = im
                rhs[c, lower, :LANES] = -im
                rhs[c, lower, LANES:] = re

        loop(0, STN // per_step, unpack)

        def detect(c):
            beam = jnp.dot(weights[g * CPG + c], rhs[c], preferred_element_type=jnp.float32)
            re = beam[:, :LANES]
            im = beam[:, LANES:]
            square = (re * re + im * im) * (1.0 / 512)
            power[g * CPG + c] = square[:B, :KS]
            pltpu.make_async_copy(power.at[g * CPG + c], out_ref.at[g * CPG + c], out_sem).start()

        loop(0, CPG, detect)

    for g in range(GROUPS):
        pltpu.make_async_copy(msg.at[g, 0 : STN - 1], recv.at[g, 0 : STN - 1], send_sem.at[g]).wait()

    @pl.when(tm > 0)
    def _():
        halo(tm).wait_send()

    pltpu.make_async_copy(power, out_ref, out_sem).wait()


def beams(main, delay, frac, taps, table, offset, index):
    vmem = pl.BlockSpec(memory_space=pltpu.VMEM)
    smem = pl.BlockSpec(memory_space=pltpu.SMEM)
    own = C // STN
    return pl.pallas_call(
        kernel,
        out_shape=jax.ShapeDtypeStruct((own, B, KS), jnp.float32),
        in_specs=[vmem, smem, smem, vmem, vmem, vmem, vmem],
        out_specs=pl.BlockSpec(memory_space=pl.ANY),
        scratch_shapes=[
            pltpu.VMEM((2, ST, EXT_COLS * LANES), jnp.bfloat16),
            pltpu.VMEM((2, ST, DCOLS * LANES), jnp.float32),
            pltpu.VMEM((KS * ST, 2 * C), jnp.bfloat16),
            pltpu.VMEM((GROUPS, STN, KG, ST, LANES), jnp.bfloat16),
            pltpu.VMEM((GROUPS, STN, KG, ST, LANES), jnp.bfloat16),
            pltpu.VMEM((own, 512, 1024), jnp.bfloat16),
            pltpu.VMEM((CPG, 1024, 2 * LANES), jnp.bfloat16),
            pltpu.VMEM((own, B, KS), jnp.float32),
            pltpu.SemaphoreType.DMA((GROUPS,)),
            pltpu.SemaphoreType.DMA((GROUPS,)),
            pltpu.SemaphoreType.DMA((GROUPS,)),
            pltpu.SemaphoreType.DMA((2,)),
            pltpu.SemaphoreType.DMA,
        ],
        compiler_params=pltpu.CompilerParams(collective_id=0, has_side_effects=True, vmem_limit_bytes=56 << 20),
    )(main, delay, frac, taps, table, offset, index)


def local(samples, filter_taps, frac_delay, station_delay, beam_index):
    main = samples.transpose(1, 0, 2)
    table = jnp.asarray(dft_columns())
    offset = jnp.asarray((column_channels() - C // 2).astype(np.float32) / C)
    return beams(main, station_delay, frac_delay, filter_taps, table, offset, beam_index)


def solution(mesh):
    in_specs = (P("stn", None, "tm"), P(), P("stn"), P("stn"), P())
    out_specs = P("stn", None, "tm")
    return jax.shard_map(local, mesh=mesh, in_specs=in_specs, out_specs=out_specs, check_vma=False)
```

time: 113 us -> 88.3 us (0.78)
  the two profiles are of different devices: /device:TPU:57 before, /device:TPU:25 now
where the time goes in v2:
time: 88.3 us; the launch traced here: 88.1 us
  Pallas kernels  81.5 us (92%)
  local copies, waits for them, and re-layouts  6.67 us (8%)
    pallas_call x1, Pallas kernels, beams(): pl.pallas_call(kernel, out_shape=jax.ShapeDtypeStruct((own, B, KS), jnp.f...  81.5 us
    unnamed x1, local copies, waits for them, and re-layouts  3.39 us
    pallas_call x1, local copies, waits for them, and re-layouts, beams(): pl.pallas_call(kernel, out_shape=jax.ShapeDtypeStruct((own, B, KS), jnp.f...  3.28 us

profile of v2, /device:TPU:25, one launch (start us, length us, event | category | flops | bytes accessed | tf_op | source)
XLA Modules:
  0.0 88.1 jit_solution(5619041234744591443)
XLA Ops:
  0.0 3.4 %copy.11 = bf16[16,2,30720]{2,0,1:T(8,128)(2,1)} copy(bf16[16,2,30720]{2,1,0:T(2,128)(2,1)} %param.7) | data formatting | bytes 3932160 | tf_op args[0]
  3.4 81.5 %shard_map.73 = f32[12,500,80]{2,1,0:T(8,128)} custom-call(bf16[2,16,30720]{2,1,0:T(8,128)(2,1)} %bitcast.3, s32[16]{0:T(128)} %delay_ref.1, f32[16]{0:T(128)} %frac_ref.1, f32[16,384]{1,0:T(8,128)} %taps_ref.1, bf16[3,768,256]{2,1,0:T(8,128)(2,1)} %constant.4.clone.table_ref, f32[3,128]{1,0:T(4,128)} %constant.5.clone.offset_ref, s32[500,512]{1,0:T(8,128)} %index_ref.1), custom_call_target="tpu_custom_call" | custom-call | tf_op jit(solution)/shard_map/pallas_call | solution.py:287
  84.9 3.3 %copy.9 = f32[12,500,80]{1,2,0:T(8,128)} copy(f32[12,500,80]{2,1,0:T(8,128)} %shard_map.73) | data formatting | bytes 3840000 | tf_op jit(solution)/shard_map/pallas_call | solution.py:287

commit v3 on v2

--- a/solution.py
+++ b/solution.py
@@ -29,6 +29,8 @@
 RIM = (TAPS - 1) * COLS + 48 * PHASES[-1][0]
 RIM_COLS = SPAN // LANES - RIM
 EXT_COLS = DCOLS + 16 - RIM
+RELAYS = 3
+PIECE = REACH // RELAYS
 MESH = pl.DeviceIdType.MESH
 
 
@@ -88,7 +90,7 @@
     return out
 
 
-def kernel(main_ref, delay_ref, frac_ref, taps_ref, table_ref, offset_ref, index_ref, out_ref, ext, dly, frames, msg, recv, weights, rhs, power, send_sem, recv_sem, own_sem, halo_sem, out_sem):
+def kernel(main_ref, delay_ref, frac_ref, taps_ref, table_ref, offset_ref, index_ref, out_ref, ext, dly, frames, msg, recv, weights, rhs, relay, send_sem, recv_sem, own_sem, halo_sem, relay_sem, edge_sem):
     me = lax.axis_index("stn")
     tm = lax.axis_index("tm")
     count = lax.axis_size("tm")
@@ -99,7 +101,22 @@
         return 0
 
     lax.fori_loop(1, STN, greet, 0)
-    pl.semaphore_signal(barrier, inc=1, device_id={"tm": lax.rem(tm + 1, count)}, device_id_type=MESH)
+    half = count // 2
+    edge = half - 1
+    far, near = count - RELAYS, half - RELAYS
+    plain_from = (tm < count - 1) & (tm != edge)
+    plain_to = (tm > 0) & (tm != half)
+
+    def greet_tm(condition, to):
+        @pl.when(condition)
+        def _():
+            pl.semaphore_signal(barrier, inc=1, device_id={"tm": to}, device_id_type=MESH)
+
+    greet_tm(plain_from, tm + 1)
+    greet_tm(tm >= far, half)
+    greet_tm((tm >= near) & (tm < half), tm + half)
+    for i in range(RELAYS - 1):
+        greet_tm(tm == edge, near + i)
 
     delay = station_rows(delay_ref)
     frac = station_rows(frac_ref)
@@ -112,7 +129,9 @@
     ext[:, :, : RIM_COLS * LANES] = main_ref[:, :, RIM * LANES :]
     ext[:, :, RIM_COLS * LANES + REACH :] = jnp.zeros((2, ST, EXT_COLS * LANES - RIM_COLS * LANES - REACH), jnp.bfloat16)
 
-    pl.semaphore_wait(barrier, STN)
+    others = plain_to.astype(jnp.int32) + (tm >= far).astype(jnp.int32)
+    others = others + ((tm >= near) & (tm < edge)).astype(jnp.int32) + (tm == half).astype(jnp.int32) * RELAYS
+    pl.semaphore_wait(barrier, STN - 1 + others)
 
     def halo(to):
         return pltpu.make_async_remote_copy(
@@ -124,7 +143,32 @@
             device_id_type=MESH,
         )
 
-    @pl.when(tm > 0)
+    def piece(source, target, to, end, start):
+        return pltpu.make_async_remote_copy(
+            src_ref=source,
+            dst_ref=target,
+            send_sem=start,
+            recv_sem=end,
+            device_id={"tm": to},
+            device_id_type=MESH,
+        )
+
+    def leave(i):
+        return piece(main_ref.at[:, :, i * PIECE : (i + 1) * PIECE], relay, far + i, relay_sem.at[0], edge_sem.at[RELAYS + i])
+
+    def cross():
+        return piece(relay, relay, tm - half, relay_sem.at[0], relay_sem.at[1])
+
+    def arrive(i, to):
+        at = RIM_COLS * LANES + i * PIECE
+        return piece(relay, ext.at[:, :, at : at + PIECE], to, edge_sem.at[i], relay_sem.at[1])
+
+    @pl.when(tm == half)
+    def _():
+        for i in range(RELAYS):
+            leave(i).start()
+
+    @pl.when(plain_to)
     def _():
         halo(tm - 1).start()
 
@@ -177,20 +221,25 @@
         for d in range(STN):
             msg[g, d, kg] = blocks[d]
 
-    def loop(start, stop, step):
+    def loop(start, stop, step, unroll=1):
         def body(i, _):
             step(i)
             return 0
 
-        lax.fori_loop(start, stop, body, 0)
+        lax.fori_loop(start, stop, body, 0, unroll=unroll)
 
     loop(0, 48 // CHUNK, lambda i: align(main_ref, i * CHUNK, 0))
     for number, (begin, end) in enumerate(PHASES):
         last = number == len(PHASES) - 1
         if last:
-            @pl.when(tm < count - 1)
+            @pl.when(plain_from)
             def _():
                 halo(tm).wait_recv()
+
+            @pl.when(tm == edge)
+            def _():
+                for i in range(RELAYS):
+                    arrive(i, tm).wait_recv()
 
         source, shift = (ext, RIM) if last else (main_ref, 0)
         first_col = (TAPS - 1) * COLS + 48 * begin
@@ -217,6 +266,24 @@
             if last:
                 pltpu.make_async_copy(msg.at[g, me], recv.at[g, me], own_sem.at[g]).start()
 
+        if number == 0:
+            @pl.when((tm >= far) & (tm < count - 1))
+            def _():
+                cross().wait_recv()
+                cross().start()
+
+            @pl.when(tm == count - 1)
+            def _():
+                cross().wait_recv()
+                arrive(RELAYS - 1, edge).start()
+
+        if number == 1:
+            for i in range(RELAYS - 1):
+                @pl.when(tm == near + i)
+                def _():
+                    cross().wait_recv()
+                    arrive(i, edge).start()
+
     own = C // STN
     first = (me * own - C // 2).astype(jnp.float32)
 
@@ -239,7 +306,7 @@
     tail = B // 16 * 16
     weigh(tail, jnp.concatenate([index_ref[tail:, :], jnp.zeros((16 - B % 16, 512), jnp.int32)], axis=0))
 
-    per_step = 4
+    per_step = 2
     wide = lax.broadcasted_iota(jnp.int32, (per_step * ST, LANES), 1)
     zero = jnp.zeros((per_step * ST, LANES), jnp.bfloat16)
     for g in range(GROUPS):
@@ -258,26 +325,32 @@
                 rhs[c, lower, :LANES] = -im
                 rhs[c, lower, LANES:] = re
 
-        loop(0, STN // per_step, unpack)
+        loop(0, STN // per_step, unpack, 4)
 
         def detect(c):
             beam = jnp.dot(weights[g * CPG + c], rhs[c], preferred_element_type=jnp.float32)
             re = beam[:, :LANES]
             im = beam[:, LANES:]
             square = (re * re + im * im) * (1.0 / 512)
-            power[g * CPG + c] = square[:B, :KS]
-            pltpu.make_async_copy(power.at[g * CPG + c], out_ref.at[g * CPG + c], out_sem).start()
+            out_ref[g * CPG + c] = square.T[:KS, :B]
 
         loop(0, CPG, detect)
 
     for g in range(GROUPS):
         pltpu.make_async_copy(msg.at[g, 0 : STN - 1], recv.at[g, 0 : STN - 1], send_sem.at[g]).wait()
 
-    @pl.when(tm > 0)
+    @pl.when(plain_to)
     def _():
         halo(tm).wait_send()
 
-    pltpu.make_async_copy(power, out_ref, out_sem).wait()
+    @pl.when(tm == half)
+    def _():
+        for i in range(RELAYS):
+            leave(i).wait_send()
+
+    @pl.when((tm >= far) | ((tm >= near) & (tm < edge)))
+    def _():
+        cross().wait_send()
 
 
 def beams(main, delay, frac, taps, table, offset, index):
@@ -286,9 +359,9 @@
     own = C // STN
     return pl.pallas_call(
         kernel,
-        out_shape=jax.ShapeDtypeStruct((own, B, KS), jnp.float32),
+        out_shape=jax.ShapeDtypeStruct((own, KS, B), jnp.float32),
         in_specs=[vmem, smem, smem, vmem, vmem, vmem, vmem],
-        out_specs=pl.BlockSpec(memory_space=pl.ANY),
+        out_specs=vmem,
         scratch_shapes=[
             pltpu.VMEM((2, ST, EXT_COLS * LANES), jnp.bfloat16),
             pltpu.VMEM((2, ST, DCOLS * LANES), jnp.float32),
@@ -297,14 +370,15 @@
             pltpu.VMEM((GROUPS, STN, KG, ST, LANES), jnp.bfloat16),
             pltpu.VMEM((own, 512, 1024), jnp.bfloat16),
             pltpu.VMEM((CPG, 1024, 2 * LANES), jnp.bfloat16),
-            pltpu.VMEM((own, B, KS), jnp.float32),
+            pltpu.VMEM((2, ST, PIECE), jnp.bfloat16),
             pltpu.SemaphoreType.DMA((GROUPS,)),
             pltpu.SemaphoreType.DMA((GROUPS,)),
             pltpu.SemaphoreType.DMA((GROUPS,)),
             pltpu.SemaphoreType.DMA((2,)),
-            pltpu.SemaphoreType.DMA,
+            pltpu.SemaphoreType.DMA((2,)),
+            pltpu.SemaphoreType.DMA((2 * RELAYS,)),
         ],
-        compiler_params=pltpu.CompilerParams(collective_id=0, has_side_effects=True, vmem_limit_bytes=56 << 20),
+        compiler_params=pltpu.CompilerParams(collective_id=0, has_side_effects=True, vmem_limit_bytes=42 << 20),
     )(main, delay, frac, taps, table, offset, index)
 
 
@@ -312,7 +386,7 @@
     main = samples.transpose(1, 0, 2)
     table = jnp.asarray(dft_columns())
     offset = jnp.asarray((column_channels() - C // 2).astype(np.float32) / C)
-    return beams(main, station_delay, frac_delay, filter_taps, table, offset, beam_index)
+    return beams(main, station_delay, frac_delay, filter_taps, table, offset, beam_index).transpose(0, 2, 1)
 
 
 def solution(mesh):

time: 88.3 us -> 68.9 us (0.78)
  the two profiles are of different devices: /device:TPU:25 before, /device:TPU:57 now
where the time goes in v3:
time: 68.9 us; the launch traced here: 68.8 us
  Pallas kernels  65.1 us (94%)
  local copies, waits for them, and re-layouts  3.57 us (5%)
    pallas_call x1, Pallas kernels, beams(): pl.pallas_call(kernel, out_shape=jax.ShapeDtypeStruct((own, KS, B), jnp.f...  65.1 us
    unnamed x14, local copies, waits for them, and re-layouts  3.57 us

profile of v3, /device:TPU:57, one launch (start us, length us, event | category | flops | bytes accessed | tf_op | source)
XLA Modules:
  0.0 68.8 jit_solution(14696370857577169849)
XLA Ops:
  0.0 0.0 copy-start
  0.0 0.0 copy-start.3
  0.0 0.0 copy-start.1
  0.0 0.0 copy-start.4
  0.0 0.0 copy-start.5
  0.0 0.0 copy-start.2
  0.0 2.3 %copy.10 = bf16[16,2,30720]{2,0,1:T(8,128)(2,1)S(1)} copy(bf16[16,2,30720]{2,1,0:T(2,128)(2,1)} %param.7) | data formatting | bytes 3932160 | tf_op args[0]
  2.3 0.0 copy-done
  2.3 0.0 copy-done.3
  2.3 0.0 copy-done.1
  2.3 0.0 copy-done.4
  2.4 0.0 copy-done.5
  2.4 0.0 copy-done.2
  2.4 65.1 %shard_map.73 = f32[12,80,500]{2,1,0:T(8,128)S(1)} custom-call(bf16[2,16,30720]{2,1,0:T(8,128)(2,1)S(1)} %bitcast.5, s32[16]{0:T(128)S(1)} %copy-done.4, f32[16]{0:T(128)S(1)} %copy-done.5, f32[16,384]{1,0:T(8,128)S(1)} %copy-done.2, bf16[3,768,256]{2,1,0:T(8,128)(2,1)S(1)} %copy-done, f32[3,128]{1,0:T(4,128)S(1)} %copy-done.3, s32[500,512]{1,0:T(8,128)S(1)} %copy-done.1), custom_call_target="tpu_custom_call" | custom-call | tf_op jit(solution)/shard_map/pallas_call | solution.py:360
  67.5 1.3 %copy.12 = f32[12,500,80]{1,2,0:T(8,128)} copy(f32[12,500,80]{1,2,0:T(8,128)S(1)} %bitcast.4) | data formatting | bytes 3840000
Async XLA Ops:
  0.0 2.3 %copy-start = (bf16[3,768,256]{2,1,0:T(8,128)(2,1)S(1)}, bf16[3,768,256]{2,1,0:T(8,128)(2,1)}, u32[]{:S(2)}) copy-start(bf16[3,768,256]{2,1,0:T(8,128)(2,1)} %constant.4.clone.table_ref) | copy-start | bytes 3538948
  0.0 2.3 %copy-start.3 = (f32[3,128]{1,0:T(4,128)S(1)}, f32[3,128]{1,0:T(4,128)}, u32[]{:S(2)}) copy-start(f32[3,128]{1,0:T(4,128)} %constant.5.clone.offset_ref) | copy-start | bytes 4612
  0.0 2.3 %copy-start.1 = (s32[500,512]{1,0:T(8,128)S(1)}, s32[500,512]{1,0:T(8,128)}, u32[]{:S(2)}) copy-start(s32[500,512]{1,0:T(8,128)} %index_ref.1) | copy-start | bytes 3072004
  0.0 2.3 %copy-start.4 = (s32[16]{0:T(128)S(1)}, s32[16]{0:T(128)}, u32[]{:S(2)}) copy-start(s32[16]{0:T(128)} %delay_ref.1) | copy-start | bytes 196
  0.0 2.3 %copy-start.5 = (f32[16]{0:T(128)S(1)}, f32[16]{0:T(128)}, u32[]{:S(2)}) copy-start(f32[16]{0:T(128)} %frac_ref.1) | copy-start | bytes 196
  0.0 2.3 %copy-start.2 = (f32[16,384]{1,0:T(8,128)S(1)}, f32[16,384]{1,0:T(8,128)}, u32[]{:S(2)}) copy-start(f32[16,384]{1,0:T(8,128)} %taps_ref.1) | copy-start | bytes 73732

commit v4 on v3

--- a/solution.py
+++ b/solution.py
@@ -29,8 +29,9 @@
 RIM = (TAPS - 1) * COLS + 48 * PHASES[-1][0]
 RIM_COLS = SPAN // LANES - RIM
 EXT_COLS = DCOLS + 16 - RIM
-RELAYS = 3
-PIECE = REACH // RELAYS
+RELAYS = 5
+CUTS = [REACH // LANES * i // RELAYS * LANES for i in range(RELAYS + 1)]
+PIECE = max(b - a for a, b in zip(CUTS, CUTS[1:]))
 MESH = pl.DeviceIdType.MESH
 
 
@@ -90,7 +91,7 @@
     return out
 
 
-def kernel(main_ref, delay_ref, frac_ref, taps_ref, table_ref, offset_ref, index_ref, out_ref, ext, dly, frames, msg, recv, weights, rhs, relay, send_sem, recv_sem, own_sem, halo_sem, relay_sem, edge_sem):
+def kernel(main_ref, delay_ref, frac_ref, taps_ref, table_ref, offset_ref, index_ref, out_ref, ext, dly, frames, msg, recv, weights, rhs, relay, send_sem, recv_sem, own_sem, halo_sem, relay_sem, edge_sem, ready_sem):
     me = lax.axis_index("stn")
     tm = lax.axis_index("tm")
     count = lax.axis_size("tm")
@@ -113,10 +114,10 @@
             pl.semaphore_signal(barrier, inc=1, device_id={"tm": to}, device_id_type=MESH)
 
     greet_tm(plain_from, tm + 1)
-    greet_tm(tm >= far, half)
     greet_tm((tm >= near) & (tm < half), tm + half)
-    for i in range(RELAYS - 1):
-        greet_tm(tm == edge, near + i)
+    greet_tm((tm >= near) & (tm < edge), edge)
+    for i in range(RELAYS):
+        greet_tm(tm == half, far + i)
 
     delay = station_rows(delay_ref)
     frac = station_rows(frac_ref)
@@ -129,8 +130,7 @@
     ext[:, :, : RIM_COLS * LANES] = main_ref[:, :, RIM * LANES :]
     ext[:, :, RIM_COLS * LANES + REACH :] = jnp.zeros((2, ST, EXT_COLS * LANES - RIM_COLS * LANES - REACH), jnp.bfloat16)
 
-    others = plain_to.astype(jnp.int32) + (tm >= far).astype(jnp.int32)
-    others = others + ((tm >= near) & (tm < edge)).astype(jnp.int32) + (tm == half).astype(jnp.int32) * RELAYS
+    others = plain_to.astype(jnp.int32) + (tm >= far).astype(jnp.int32) * 2 + (tm == edge).astype(jnp.int32) * (RELAYS - 1)
     pl.semaphore_wait(barrier, STN - 1 + others)
 
     def halo(to):
@@ -154,19 +154,27 @@
         )
 
     def leave(i):
-        return piece(main_ref.at[:, :, i * PIECE : (i + 1) * PIECE], relay, far + i, relay_sem.at[0], edge_sem.at[RELAYS + i])
-
-    def cross():
-        return piece(relay, relay, tm - half, relay_sem.at[0], relay_sem.at[1])
-
-    def arrive(i, to):
-        at = RIM_COLS * LANES + i * PIECE
-        return piece(relay, ext.at[:, :, at : at + PIECE], to, edge_sem.at[i], relay_sem.at[1])
-
-    @pl.when(tm == half)
-    def _():
-        for i in range(RELAYS):
-            leave(i).start()
+        width = CUTS[i + 1] - CUTS[i]
+        source = main_ref.at[:, :, CUTS[i] : CUTS[i + 1]]
+        return piece(source, relay.at[:, :, :width], far + i, relay_sem.at[0], edge_sem.at[RELAYS + i])
+
+    def cross(i):
+        part = relay.at[:, :, : CUTS[i + 1] - CUTS[i]]
+        return piece(part, part, near + i, relay_sem.at[0], relay_sem.at[1])
+
+    def arrive(i):
+        at = RIM_COLS * LANES
+        target = ext.at[:, :, at + CUTS[i] : at + CUTS[i + 1]]
+        return piece(relay.at[:, :, : CUTS[i + 1] - CUTS[i]], target, edge, edge_sem.at[i], relay_sem.at[1])
+
+    def ready(condition, to):
+        @pl.when(condition)
+        def _():
+            pl.semaphore_signal(ready_sem, inc=1, device_id={"tm": to}, device_id_type=MESH)
+
+    ready(tm >= far, half)
+    for i in range(RELAYS - 1):
+        ready(tm == edge, near + i)
 
     @pl.when(plain_to)
     def _():
@@ -239,7 +247,7 @@
             @pl.when(tm == edge)
             def _():
                 for i in range(RELAYS):
-                    arrive(i, tm).wait_recv()
+                    arrive(i).wait_recv()
 
         source, shift = (ext, RIM) if last else (main_ref, 0)
         first_col = (TAPS - 1) * COLS + 48 * begin
@@ -267,22 +275,25 @@
                 pltpu.make_async_copy(msg.at[g, me], recv.at[g, me], own_sem.at[g]).start()
 
         if number == 0:
-            @pl.when((tm >= far) & (tm < count - 1))
+            @pl.when(tm == half)
             def _():
-                cross().wait_recv()
-                cross().start()
-
-            @pl.when(tm == count - 1)
-            def _():
-                cross().wait_recv()
-                arrive(RELAYS - 1, edge).start()
+                pl.semaphore_wait(ready_sem, RELAYS)
+                for i in range(RELAYS):
+                    leave(i).start()
+
+            for i in range(RELAYS):
+                @pl.when(tm == far + i)
+                def _():
+                    cross(i).wait_recv()
+                    (cross(i) if i < RELAYS - 1 else arrive(i)).start()
 
         if number == 1:
             for i in range(RELAYS - 1):
                 @pl.when(tm == near + i)
                 def _():
-                    cross().wait_recv()
-                    arrive(i, edge).start()
+                    pl.semaphore_wait(ready_sem, 1)
+                    cross(i).wait_recv()
+                    arrive(i).start()
 
     own = C // STN
     first = (me * own - C // 2).astype(jnp.float32)
@@ -348,9 +359,10 @@
         for i in range(RELAYS):
             leave(i).wait_send()
 
-    @pl.when((tm >= far) | ((tm >= near) & (tm < edge)))
-    def _():
-        cross().wait_send()
+    for i in range(RELAYS):
+        @pl.when((tm == far + i) | (tm == near + i) & (tm < edge))
+        def _():
+            cross(i).wait_send()
 
 
 def beams(main, delay, frac, taps, table, offset, index):
@@ -377,6 +389,7 @@
             pltpu.SemaphoreType.DMA((2,)),
             pltpu.SemaphoreType.DMA((2,)),
             pltpu.SemaphoreType.DMA((2 * RELAYS,)),
+            pltpu.SemaphoreType.REGULAR,
         ],
         compiler_params=pltpu.CompilerParams(collective_id=0, has_side_effects=True, vmem_limit_bytes=42 << 20),
     )(main, delay, frac, taps, table, offset, index)

time: 68.9 us -> 65.7 us (0.954)
  the two profiles are of different devices: /device:TPU:57 before, /device:TPU:1 now
where the time goes in v4:
time: 65.7 us; the launch traced here: 65.6 us
  Pallas kernels  61.9 us (94%)
  local copies, waits for them, and re-layouts  3.57 us (5%)
    pallas_call x1, Pallas kernels, beams(): pl.pallas_call(kernel, out_shape=jax.ShapeDtypeStruct((own, KS, B), jnp.f...  61.9 us
    unnamed x14, local copies, waits for them, and re-layouts  3.57 us

profile of v4, /device:TPU:1, one launch (start us, length us, event | category | flops | bytes accessed | tf_op | source)
XLA Modules:
  0.0 65.6 jit_solution(6152553160410203588)
XLA Ops:
  0.0 0.0 copy-start
  0.0 0.0 copy-start.3
  0.0 0.0 copy-start.1
  0.0 0.0 copy-start.4
  0.0 0.0 copy-start.5
  0.0 0.0 copy-start.2
  0.0 2.3 %copy.10 = bf16[16,2,30720]{2,0,1:T(8,128)(2,1)S(1)} copy(bf16[16,2,30720]{2,1,0:T(2,128)(2,1)} %param.7) | data formatting | bytes 3932160 | tf_op args[0]
  2.3 0.0 copy-done
  2.3 0.0 copy-done.3
  2.3 0.0 copy-done.1
  2.3 0.0 copy-done.4
  2.4 0.0 copy-done.5
  2.4 0.0 copy-done.2
  2.4 61.9 %shard_map.73 = f32[12,80,500]{2,1,0:T(8,128)S(1)} custom-call(bf16[2,16,30720]{2,1,0:T(8,128)(2,1)S(1)} %bitcast.5, s32[16]{0:T(128)S(1)} %copy-done.4, f32[16]{0:T(128)S(1)} %copy-done.5, f32[16,384]{1,0:T(8,128)S(1)} %copy-done.2, bf16[3,768,256]{2,1,0:T(8,128)(2,1)S(1)} %copy-done, f32[3,128]{1,0:T(4,128)S(1)} %copy-done.3, s32[500,512]{1,0:T(8,128)S(1)} %copy-done.1), custom_call_target="tpu_custom_call" | custom-call | tf_op jit(solution)/shard_map/pallas_call | solution.py:372
  64.3 1.3 %copy.12 = f32[12,500,80]{1,2,0:T(8,128)} copy(f32[12,500,80]{1,2,0:T(8,128)S(1)} %bitcast.4) | data formatting | bytes 3840000
Async XLA Ops:
  0.0 2.3 %copy-start = (bf16[3,768,256]{2,1,0:T(8,128)(2,1)S(1)}, bf16[3,768,256]{2,1,0:T(8,128)(2,1)}, u32[]{:S(2)}) copy-start(bf16[3,768,256]{2,1,0:T(8,128)(2,1)} %constant.4.clone.table_ref) | copy-start | bytes 3538948
  0.0 2.3 %copy-start.3 = (f32[3,128]{1,0:T(4,128)S(1)}, f32[3,128]{1,0:T(4,128)}, u32[]{:S(2)}) copy-start(f32[3,128]{1,0:T(4,128)} %constant.5.clone.offset_ref) | copy-start | bytes 4612
  0.0 2.3 %copy-start.1 = (s32[500,512]{1,0:T(8,128)S(1)}, s32[500,512]{1,0:T(8,128)}, u32[]{:S(2)}) copy-start(s32[500,512]{1,0:T(8,128)} %index_ref.1) | copy-start | bytes 3072004
  0.0 2.3 %copy-start.4 = (s32[16]{0:T(128)S(1)}, s32[16]{0:T(128)}, u32[]{:S(2)}) copy-start(s32[16]{0:T(128)} %delay_ref.1) | copy-start | bytes 196
  0.0 2.3 %copy-start.5 = (f32[16]{0:T(128)S(1)}, f32[16]{0:T(128)}, u32[]{:S(2)}) copy-start(f32[16]{0:T(128)} %frac_ref.1) | copy-start | bytes 196
  0.0 2.3 %copy-start.2 = (f32[16,384]{1,0:T(8,128)S(1)}, f32[16,384]{1,0:T(8,128)}, u32[]{:S(2)}) copy-start(f32[16,384]{1,0:T(8,128)} %taps_ref.1) | copy-start | bytes 73732

commit v5 on v4

--- a/solution.py
+++ b/solution.py
@@ -345,7 +345,7 @@
             square = (re * re + im * im) * (1.0 / 512)
             out_ref[g * CPG + c] = square.T[:KS, :B]
 
-        loop(0, CPG, detect)
+        loop(0, CPG, detect, CPG)
 
     for g in range(GROUPS):
         pltpu.make_async_copy(msg.at[g, 0 : STN - 1], recv.at[g, 0 : STN - 1], send_sem.at[g]).wait()

time: 65.7 us -> 64.1 us (0.976)
  Pallas kernels: 61.9 us -> 60.3 us
    pallas_call x1, Pallas kernels: 61.9 us -> 60.3 us  [beams(): pl.pallas_call(kernel, out_shape=jax.ShapeDtypeStruct((own, KS, B), jnp.f...]
where the time goes in v5:
time: 64.1 us; the launch traced here: 64 us
  Pallas kernels  60.3 us (94%)
  local copies, waits for them, and re-layouts  3.57 us (6%)
    pallas_call x1, Pallas kernels, beams(): pl.pallas_call(kernel, out_shape=jax.ShapeDtypeStruct((own, KS, B), jnp.f...  60.3 us
    unnamed x14, local copies, waits for them, and re-layouts  3.57 us

profile of v5, /device:TPU:1, one launch (start us, length us, event | category | flops | bytes accessed | tf_op | source)
XLA Modules:
  0.0 64.0 jit_solution(2257746177117427352)
XLA Ops:
  0.0 0.0 copy-start
  0.0 0.0 copy-start.3
  0.0 0.0 copy-start.1
  0.0 0.0 copy-start.4
  0.0 0.0 copy-start.5
  0.0 0.0 copy-start.2
  0.0 2.3 %copy.10 = bf16[16,2,30720]{2,0,1:T(8,128)(2,1)S(1)} copy(bf16[16,2,30720]{2,1,0:T(2,128)(2,1)} %param.7) | data formatting | bytes 3932160 | tf_op args[0]
  2.3 0.0 copy-done
  2.3 0.0 copy-done.3
  2.3 0.0 copy-done.1
  2.3 0.0 copy-done.4
  2.4 0.0 copy-done.5
  2.4 0.0 copy-done.2
  2.4 60.3 %shard_map.73 = f32[12,80,500]{2,1,0:T(8,128)S(1)} custom-call(bf16[2,16,30720]{2,1,0:T(8,128)(2,1)S(1)} %bitcast.5, s32[16]{0:T(128)S(1)} %copy-done.4, f32[16]{0:T(128)S(1)} %copy-done.5, f32[16,384]{1,0:T(8,128)S(1)} %copy-done.2, bf16[3,768,256]{2,1,0:T(8,128)(2,1)S(1)} %copy-done, f32[3,128]{1,0:T(4,128)S(1)} %copy-done.3, s32[500,512]{1,0:T(8,128)S(1)} %copy-done.1), custom_call_target="tpu_custom_call" | custom-call | tf_op jit(solution)/shard_map/pallas_call | solution.py:372
  62.7 1.3 %copy.12 = f32[12,500,80]{1,2,0:T(8,128)} copy(f32[12,500,80]{1,2,0:T(8,128)S(1)} %bitcast.4) | data formatting | bytes 3840000
Async XLA Ops:
  0.0 2.3 %copy-start = (bf16[3,768,256]{2,1,0:T(8,128)(2,1)S(1)}, bf16[3,768,256]{2,1,0:T(8,128)(2,1)}, u32[]{:S(2)}) copy-start(bf16[3,768,256]{2,1,0:T(8,128)(2,1)} %constant.4.clone.table_ref) | copy-start | bytes 3538948
  0.0 2.3 %copy-start.3 = (f32[3,128]{1,0:T(4,128)S(1)}, f32[3,128]{1,0:T(4,128)}, u32[]{:S(2)}) copy-start(f32[3,128]{1,0:T(4,128)} %constant.5.clone.offset_ref) | copy-start | bytes 4612
  0.0 2.3 %copy-start.1 = (s32[500,512]{1,0:T(8,128)S(1)}, s32[500,512]{1,0:T(8,128)}, u32[]{:S(2)}) copy-start(s32[500,512]{1,0:T(8,128)} %index_ref.1) | copy-start | bytes 3072004
  0.0 2.3 %copy-start.4 = (s32[16]{0:T(128)S(1)}, s32[16]{0:T(128)}, u32[]{:S(2)}) copy-start(s32[16]{0:T(128)} %delay_ref.1) | copy-start | bytes 196
  0.0 2.3 %copy-start.5 = (f32[16]{0:T(128)S(1)}, f32[16]{0:T(128)}, u32[]{:S(2)}) copy-start(f32[16]{0:T(128)} %frac_ref.1) | copy-start | bytes 196
  0.0 2.3 %copy-start.2 = (f32[16,384]{1,0:T(8,128)S(1)}, f32[16,384]{1,0:T(8,128)}, u32[]{:S(2)}) copy-start(f32[16,384]{1,0:T(8,128)} %taps_ref.1) | copy-start | bytes 73732
